TPU v7x, 32 devices: a whole 2x2x4 slice. The times are simulated.
32 devices in a mesh: harm: 4 (over z), node: 8 (over y, x, core).
Axes of the slice: x: 2, y: 2, z: 4, core: 2. Of those that a mesh axis runs over, the one named last changes fastest.
Arguments:
- adjoint: bfloat16 [128, 4, 32768], P('harm', None, 'node'), may hold values from -6 to 6
- source: float32 [128, 131072], P(None, ('harm', 'node')), may hold values from -6 to 6
- rad_coeff: bfloat16 [128, 131072], P(None, ('harm', 'node')), may hold values from 0.19921875 to 2
- capacity: float32 [131072], P(('harm', 'node')), may hold values from 0.005 to 0.03
- inv_diag: float32 [131072], P(('harm', 'node')), may hold values from 0.1 to 0.5
- blocks: bfloat16 [1024, 4, 128, 128], P(('harm', 'node')), may hold values from -0.25 to 0.25
- block_cols: int32 [1024, 4], P(('harm', 'node')), may hold values from 0 to 1023, as said below
- zone_of: int32 [131072], P(('harm', 'node')), may hold values from 0 to 1279, as said below
- heater_weight: float32 [131072], P(('harm', 'node')), may hold values from 0.2 to 2
Outputs:
- updated: bfloat16 [128, 4, 32768], P('harm', None, 'node')
- gradient: float32 [1280, 128], P(('harm', 'node'))
Inputs may be any that keep to these rules, and one draw needn't show every extreme that they name: `block_cols`: with d = b // 32 and D = 32: slot 0 of row block b names b itself; slot 1 lies in row blocks max(d - 1, 0) * 32 to (max(d - 1, 0) + 1) * 32 - 1; slot 2 in min(d + 1, D - 1) * 32 to (min(d + 1, D - 1) + 1) * 32 - 1; the other slots in (d - 1) * 32 to (d + 2) * 32 - 1. `zone_of`: node n lies in a zone z with (n // 4096 - 1) * 40 <= z < (n // 4096 + 2) * 40.
All inputs are finite; a program needn't handle non-finite values.
Results may differ from a plain program's by a relative error of at most 0.0035.
Values may be sent and summed in bfloat16 or wider, within the bound.
A program may use at most 64 MiB of HBM per device.

v0:
```python
import math
import jax
import jax.numpy as jnp
from jax import lax
from jax.sharding import PartitionSpec as P

ZONE_DEV = 40


def with_halo(value, sides, width):
    for axis, dim in sides:
        count, length = (lax.axis_size(axis), value.shape[dim])
        up = [(i, (i + 1) % count) for i in range(count - 1)]
        down = [(j, i) for i, j in up]
        last = lax.slice_in_dim(value, length - width, length, axis=dim)
        initial = lax.slice_in_dim(value, 0, width, axis=dim)
        before = lax.ppermute(last, axis, up)
        after = lax.ppermute(initial, axis, down)
        value = jnp.concatenate([before, value, after], axis=dim)
    return value


def passed_along(value, axis, steps):
    count = lax.axis_size(axis)
    initial, last = (max(0, -steps), min(count, count - steps))
    return lax.ppermute(value, axis, [(source, source + steps) for source in range(initial, last)])


def fourier_basis(count):
    sample_index = jnp.arange(count, dtype=jnp.float32)[:, None]
    column_index = jnp.arange(count)[None, :]
    half_count = count // 2
    frequency = jnp.where(
        column_index <= half_count, column_index, column_index - half_count
    ).astype(jnp.float32)
    angle = 2.0 * math.pi * frequency * sample_index / count
    values_table = jnp.where(column_index <= half_count, jnp.cos(angle), jnp.sin(angle))
    scaling = jnp.where(
        (column_index == 0) | (column_index == half_count),
        math.sqrt(1.0 / count),
        math.sqrt(2.0 / count),
    )
    return (values_table * scaling).astype(jnp.bfloat16)


def derivative_term(field):
    half_count = field.shape[0] // 2
    wave_number = jnp.arange(1, half_count, dtype=jnp.float32)[:, None]
    zero_row = jnp.zeros((1, field.shape[1]), jnp.float32)
    upper_rows = wave_number * field[half_count + 1 :]
    lower_rows = -wave_number * field[1:half_count]
    return jnp.concatenate([zero_row, upper_rows, zero_row, lower_rows], axis=0)


def body(
    adjoint, source, rad_coeff, capacity, inv_diag, blocks, block_cols, zone_of, heater_weight
):
    arrived = lax.all_to_all(adjoint, "harm", split_axis=1, concat_axis=0, tiled=True)
    harmonics = arrived.shape[0]
    node_count = arrived.shape[2]
    field = arrived.reshape(harmonics, node_count)
    block_size = blocks.shape[2]
    row_blocks = node_count // block_size
    fourier = fourier_basis(harmonics)
    samples = jnp.dot(fourier, field, preferred_element_type=jnp.float32)
    weighted = (rad_coeff.astype(jnp.float32) * samples).astype(jnp.bfloat16)
    radiative = jnp.dot(fourier.T, weighted, preferred_element_type=jnp.float32)
    rate_term = derivative_term(field.astype(jnp.float32))
    padded = with_halo(field, ((("harm", "node"), 1),), node_count)
    position = lax.axis_index(("harm", "node"))
    local_cols = block_cols - (position - 1) * row_blocks
    extended = padded.reshape(harmonics, 3 * row_blocks, block_size)
    gathered = jnp.take(extended, local_cols, axis=1)
    conduction = jnp.einsum(
        "kbsj,bsij->kbi", gathered, blocks, preferred_element_type=jnp.float32
    ).reshape(harmonics, node_count)
    residual = source - (capacity[None, :] * rate_term + conduction + radiative)
    updated = (field.astype(jnp.float32) + inv_diag[None, :] * residual).astype(jnp.bfloat16)
    returned = lax.all_to_all(
        updated.reshape(harmonics, 1, node_count), "harm", split_axis=0, concat_axis=1, tiled=True
    )
    weighted_terms = (updated.astype(jnp.float32) * heater_weight[None, :]).T
    window_zone = zone_of - (position - 1) * ZONE_DEV
    selector = (window_zone[:, None] == jnp.arange(3 * ZONE_DEV, dtype=jnp.int32)[None, :]).astype(
        jnp.float32
    )
    window_sums = jnp.einsum("nz,nk->zk", selector, weighted_terms, precision=lax.Precision.HIGHEST)
    lower_part = window_sums[:ZONE_DEV]
    middle_part = window_sums[ZONE_DEV : 2 * ZONE_DEV]
    upper_part = window_sums[2 * ZONE_DEV :]
    above_terms = passed_along(lower_part, ("harm", "node"), -1)
    below_terms = passed_along(upper_part, ("harm", "node"), 1)
    gradient = middle_part + above_terms + below_terms
    return (returned, gradient)


def solution(mesh):
    in_specs = (
        P("harm", None, "node"),
        P(None, ("harm", "node")),
        P(None, ("harm", "node")),
        P(("harm", "node")),
        P(("harm", "node")),
        P(("harm", "node"), None, None, None),
        P(("harm", "node"), None),
        P(("harm", "node")),
        P(("harm", "node")),
    )
    out_specs = (P("harm", None, "node"), P(("harm", "node"), None))
    return jax.shard_map(body, mesh=mesh, in_specs=in_specs, out_specs=out_specs, check_vma=False)
```

profile of v0, /device:TPU:4, one launch (start us, length us, event | category | flops | bytes accessed | tf_op | source)
XLA Modules:
  0.0 116.6 jit_solution(15993468261064862405)
XLA Ops:
  0.6 0.0 copy-start.6
  0.6 2.8 %copy.35 = bf16[32,4,4096]{2,0,1:T(8,128)(2,1)} copy(bf16[32,4,4096]{2,1,0:T(4,128)(2,1)} %param.9) | data formatting | bytes 2097152 | tf_op args[0]
  3.4 4.9 %all-to-all-start = ((bf16[32,4,4096]{2,0,1:T(8,128)(2,1)}), bf16[32,4,4096]{2,0,1:T(8,128)(2,1)S(1)}, u32[]{:S(2)}, u32[]{:S(2)}) async-start(bf16[32,4,4096]{2,0,1:T(8,128)(2,1)} %copy.35), calls=%async_computation | async-start | bytes 2097152 | tf_op jit(solution)/shard_map/all_to_all | solution.py:58
  8.3 0.0 copy-done.6
  8.3 0.1 copy.40
  8.4 0.1 reshape.72
  8.5 0.1 copy.36
  8.6 25.4 %all-to-all-done = bf16[32,4,4096]{2,0,1:T(8,128)(2,1)S(1)} async-done(((bf16[32,4,4096]{2,0,1:T(8,128)(2,1)}), bf16[32,4,4096]{2,0,1:T(8,128)(2,1)S(1)}, u32[]{:S(2)}, u32[]{:S(2)}) %all-to-all-start) | async-done | bytes 1048608 | tf_op jit(solution)/shard_map/all_to_all | solution.py:58
  34.0 0.0 copy-start
  34.0 2.0 %collective-permute-start.1 = (bf16[128,4096]{1,0:T(8,128)(2,1)S(1)}, bf16[128,4096]{1,0:T(8,128)(2,1)S(1)}, u32[]{:S(2)}, u32[]{:S(2)}) collective-permute-start(bf16[128,4096]{1,0:T(8,128)(2,1)S(1)} %bitcast.39), channel_id=1, source_target_pairs={{1,0},{2,1},{3,2},{4,3},{5,4},{6,5},{7,6},{8,7},{9,8},{10,9},{11,1... | collective-permute-start | bytes 3145736 | tf_op jit(solution)/shard_map/ppermute | solution.py:18
  36.0 2.3 %collective-permute-start = (bf16[128,4096]{1,0:T(8,128)(2,1)S(1)}, bf16[128,4096]{1,0:T(8,128)(2,1)S(1)}, u32[]{:S(2)}, u32[]{:S(2)}) collective-permute-start(bf16[128,4096]{1,0:T(8,128)(2,1)S(1)} %bitcast.40), channel_id=1, source_target_pairs={{0,1},{1,2},{2,3},{3,4},{4,5},{5,6},{6,7},{7,8},{8,9},{9,10},{10,1... | collective-permute-start | bytes 3145736 | tf_op jit(solution)/shard_map/ppermute | solution.py:17
  38.3 0.3 bitcast_convert_fusion
  38.6 0.2 copy.48
  38.9 0.0 copy-done
  38.9 0.4 copy.38
  39.3 1.6 %slice_multiply_fusion.1 = (f32[63,4096]{1,0:T(8,128)}, f32[63,4096]{1,0:T(8,128)}) fusion(f32[128,4096]{1,0:T(8,128)S(1)} %bitcast_convert_fusion, f32[63]{0:T(128)S(1)} %get-tuple-element.10, f32[63]{0:T(128)S(1)} %get-tuple-element.11), kind=kLoop, calls=%fused_computation.24 | loop fusion | flops 516096 | bytes 4129272 | tf_op jit(solution)/shard_map/mul | solution.py:50
  40.9 15.8 %collective-permute-done.1 = bf16[128,4096]{1,0:T(8,128)(2,1)S(1)} collective-permute-done((bf16[128,4096]{1,0:T(8,128)(2,1)S(1)}, bf16[128,4096]{1,0:T(8,128)(2,1)S(1)}, u32[]{:S(2)}, u32[]{:S(2)}) %collective-permute-start.1) | collective-permute-done | bytes 1048608 | tf_op jit(solution)/shard_map/ppermute | solution.py:18
  56.7 0.3 copy_bitcast_fusion
  57.0 4.3 %collective-permute-done = bf16[128,4096]{1,0:T(8,128)(2,1)S(1)} collective-permute-done((bf16[128,4096]{1,0:T(8,128)(2,1)S(1)}, bf16[128,4096]{1,0:T(8,128)(2,1)S(1)}, u32[]{:S(2)}, u32[]{:S(2)}) %collective-permute-start) | collective-permute-done | bytes 1048608 | tf_op jit(solution)/shard_map/ppermute | solution.py:17
  61.4 0.3 copy_bitcast_fusion.1
  61.6 0.4 pad_maximum_fusion
  62.0 3.0 %gather_fusion = bf16[128,128,128]{2,1,0:T(8,128)(2,1)} fusion(bf16[128,96,128]{2,0,1:T(8,128)(2,1)S(1)} %pad_maximum_fusion, s32[1024]{0:T(1024)S(1)} %pad_clamp_fusion), kind=kCustom, calls=%fused_computation | custom fusion | bytes 8389120 | tf_op jit(solution)/shard_map/jit(_take)/gather | solution.py:73
  65.1 6.2 %fusion.5 = f32[32,128,128,1]{1,2,3,0:T(8,128)} fusion(bf16[32,4,128,128]{3,2,1,0:T(8,128)(2,1)} %param.14, bf16[32,4,128,128]{3,2,1,0:T(8,128)(2,1)} %bitcast.44, pred[32,4]{1,0:T(8,128)(4,1)S(1)} %copy.36), kind=kOutput, calls=%fused_computation.8 | convolution fusion | flops 538968064 | bytes 10485888 | tf_op jit(solution)/shard_map/kbsj,bsij->kbi/dot_general | solution.py:74
  71.3 2.0 %copy.41 = f32[128,4096]{1,0:T(8,128)S(1)} copy(f32[128,4096]{0,1:T(8,128)} %bitcast.47) | data formatting | bytes 4194304 | tf_op jit(solution)/shard_map/reshape | solution.py:76
  73.3 0.0 copy-done.1
  73.3 0.0 copy-done.3
  73.3 0.0 copy-done.4
  73.3 5.2 %fusion.4 = bf16[128,4096]{1,0:T(8,128)(2,1)} fusion(f32[128,4096]{1,0:T(8,128)} %param.10, f32[128,4096]{1,0:T(8,128)S(1)} %copy.41, f32[63,4096]{1,0:T(8,128)} %get-tuple-element.7, f32[1,4096]{1,0:T(1,128)S(1)} %broadcast_in_dim.41, f32[63,4096]{1,0:T(8,128)} %get-tuple-element.6, bf16[128,4096]{1,0:T(8,128)(2,1)S(1)} %bitcast.42, ...), kind=kOutput, calls=%fused_computation.7 | convolution fusion | flops 275939328 | bytes 9454720 | tf_op jit(solution)/shard_map/dot_general | solution.py:67
  78.5 0.5 broadcast.81
  79.0 2.6 %reduce = bf16[128,4096]{1,0:T(8,128)(2,1)S(1)} reduce(bf16[128,1,4096]{2,0,1:T(8,128)(2,1)} %bitcast.46, bf16[]{:T(256)} %broadcast.81), dimensions={1}, to_apply=%copy.42.reduce_sub_computation | reduce | bytes 2097154 | tf_op jit(solution)/shard_map/reshape | solution.py:80
  81.7 0.0 copy-start.5
  81.7 0.0 copy-start.2
  81.7 0.0 copy-start.7
  81.7 2.0 %reshape.81 = bf16[4,2,65536]{2,1,0:T(2,128)(2,1)} reshape(bf16[128,4096]{1,0:T(8,128)(2,1)S(1)} %reduce) | data formatting | bytes 2097152
  83.7 3.5 %all-to-all-start.1 = ((bf16[4,2,65536]{2,1,0:T(2,128)(2,1)}), bf16[4,2,65536]{2,1,0:T(2,128)(2,1)S(1)}, u32[]{:S(2)}, u32[]{:S(2)}) async-start(bf16[4,2,65536]{2,1,0:T(2,128)(2,1)} %reshape.81), calls=%async_computation.1 | async-start | bytes 2097152 | tf_op jit(solution)/shard_map/all_to_all | solution.py:79
  87.2 0.0 copy-done.5
  87.2 0.0 copy-done.2
  87.3 0.0 copy-done.7
  87.3 2.1 %fusion.11 = f32[120,128]{1,0:T(8,128)S(1)} fusion(bf16[128,4096]{1,0:T(8,128)(2,1)S(1)} %copy-done.2, f32[4096]{0:T(1024)S(1)} %copy-done.7, s32[4096]{0:T(1024)S(1)} %broadcast_subtract_fusion), kind=kOutput, calls=%fused_computation.16 | convolution fusion | flops 757006336 | bytes 1142784 | tf_op jit(solution)/shard_map/nz,nk->zk/dot_general | solution.py:87
  89.4 1.9 %collective-permute-start.2 = (f32[40,128]{1,0:T(8,128)S(1)}, f32[40,128]{1,0:T(8,128)S(1)}, u32[]{:S(2)}, u32[]{:S(2)}) collective-permute-start(f32[40,128]{1,0:T(8,128)S(1)} %get-tuple-element.8), channel_id=1, source_target_pairs={{1,0},{2,1},{3,2},{4,3},{5,4},{6,5},{7,6},{8,7},{9,8},{10,9},{11,1... | collective-permute-start | bytes 61448 | tf_op jit(solution)/shard_map/ppermute | solution.py:26
  91.3 2.4 %collective-permute-start.3 = (f32[40,128]{1,0:T(8,128)S(1)}, f32[40,128]{1,0:T(8,128)S(1)}, u32[]{:S(2)}, u32[]{:S(2)}) collective-permute-start(f32[40,128]{1,0:T(8,128)S(1)} %get-tuple-element.9), channel_id=1, source_target_pairs={{0,1},{1,2},{2,3},{3,4},{4,5},{5,6},{6,7},{7,8},{8,9},{9,10},{10,1... | collective-permute-start | bytes 61448 | tf_op jit(solution)/shard_map/ppermute | solution.py:26
  93.7 0.0 collective-permute-done.2
  93.7 3.6 %collective-permute-done.3 = f32[40,128]{1,0:T(8,128)S(1)} collective-permute-done((f32[40,128]{1,0:T(8,128)S(1)}, f32[40,128]{1,0:T(8,128)S(1)}, u32[]{:S(2)}, u32[]{:S(2)}) %collective-permute-start.3) | collective-permute-done | bytes 20512 | tf_op jit(solution)/shard_map/ppermute | solution.py:26
  97.3 0.6 fusion.26
  97.9 14.8 %all-to-all-done.1 = bf16[4,2,65536]{2,1,0:T(2,128)(2,1)S(1)} async-done(((bf16[4,2,65536]{2,1,0:T(2,128)(2,1)}), bf16[4,2,65536]{2,1,0:T(2,128)(2,1)S(1)}, u32[]{:S(2)}, u32[]{:S(2)}) %all-to-all-start.1) | async-done | bytes 1048608 | tf_op jit(solution)/shard_map/all_to_all | solution.py:79
  112.7 0.9 reshape.82
  113.7 1.1 copy.45
  114.9 1.8 %copy.43 = bf16[32,4,4096]{2,1,0:T(4,128)(2,1)} copy(bf16[32,4,4096]{2,0,1:T(8,128)(2,1)S(1)} %bitcast.43) | data formatting | bytes 2097152
  (11 shorter events, 0.1 us)
Async XLA Ops:
  0.6 7.7 %copy-start.6 = (s32[32,4]{0,1:T(4,128)S(1)}, s32[32,4]{0,1:T(4,128)}, u32[]{:S(2)}) copy-start(s32[32,4]{0,1:T(4,128)} %param.15) | copy-start | bytes 1540
  3.4 30.6 %all-to-all-start = ((bf16[32,4,4096]{2,0,1:T(8,128)(2,1)}), bf16[32,4,4096]{2,0,1:T(8,128)(2,1)S(1)}, u32[]{:S(2)}, u32[]{:S(2)}) async-start(bf16[32,4,4096]{2,0,1:T(8,128)(2,1)} %copy.35), calls=%async_computation | async-start | bytes 2097152 | tf_op jit(solution)/shard_map/all_to_all | solution.py:58
  34.0 4.9 %copy-start = (bf16[32,4,4096]{2,0,1:T(8,128)(2,1)}, bf16[32,4,4096]{2,0,1:T(8,128)(2,1)S(1)}, u32[]{:S(2)}) copy-start(bf16[32,4,4096]{2,0,1:T(8,128)(2,1)S(1)} %all-to-all-done) | copy-start | bytes 3145732
  34.0 22.7 %collective-permute-start.1 = (bf16[128,4096]{1,0:T(8,128)(2,1)S(1)}, bf16[128,4096]{1,0:T(8,128)(2,1)S(1)}, u32[]{:S(2)}, u32[]{:S(2)}) collective-permute-start(bf16[128,4096]{1,0:T(8,128)(2,1)S(1)} %bitcast.39), channel_id=1, source_target_pairs={{1,0},{2,1},{3,2},{4,3},{5,4},{6,5},{7,6},{8,7},{9,8},{10,9},{11,1... | collective-permute-start | bytes 3145736 | tf_op jit(solution)/shard_map/ppermute | solution.py:18
  36.0 25.3 %collective-permute-start = (bf16[128,4096]{1,0:T(8,128)(2,1)S(1)}, bf16[128,4096]{1,0:T(8,128)(2,1)S(1)}, u32[]{:S(2)}, u32[]{:S(2)}) collective-permute-start(bf16[128,4096]{1,0:T(8,128)(2,1)S(1)} %bitcast.40), channel_id=1, source_target_pairs={{0,1},{1,2},{2,3},{3,4},{4,5},{5,6},{6,7},{7,8},{8,9},{9,10},{10,1... | collective-permute-start | bytes 3145736 | tf_op jit(solution)/shard_map/ppermute | solution.py:17
  71.3 2.0 %copy-start.1 = (bf16[32,4,4096]{2,0,1:T(8,128)(2,1)S(1)}, bf16[32,4,4096]{2,0,1:T(8,128)(2,1)}, u32[]{:S(2)}) copy-start(bf16[32,4,4096]{2,0,1:T(8,128)(2,1)} %copy-done) | copy-start | bytes 3145732
  71.3 2.0 %copy-start.3 = (f32[4096]{0:T(1024)S(1)}, f32[4096]{0:T(1024)}, u32[]{:S(2)}) copy-start(f32[4096]{0:T(1024)} %param.12) | copy-start | bytes 49156
  71.3 2.1 %copy-start.4 = (f32[4096]{0:T(1024)S(1)}, f32[4096]{0:T(1024)}, u32[]{:S(2)}) copy-start(f32[4096]{0:T(1024)} %param.13) | copy-start | bytes 49156
  81.7 5.6 %copy-start.5 = (s32[4096]{0:T(1024)S(1)}, s32[4096]{0:T(1024)}, u32[]{:S(2)}) copy-start(s32[4096]{0:T(1024)} %param.16) | copy-start | bytes 49156
  81.7 5.6 %copy-start.2 = (bf16[128,4096]{1,0:T(8,128)(2,1)S(1)}, bf16[128,4096]{1,0:T(8,128)(2,1)}, u32[]{:S(2)}) copy-start(bf16[128,4096]{1,0:T(8,128)(2,1)} %fusion.4) | copy-start | bytes 3145732
  81.7 5.6 %copy-start.7 = (f32[4096]{0:T(1024)S(1)}, f32[4096]{0:T(1024)}, u32[]{:S(2)}) copy-start(f32[4096]{0:T(1024)} %param.17) | copy-start | bytes 49156
  83.7 29.0 %all-to-all-start.1 = ((bf16[4,2,65536]{2,1,0:T(2,128)(2,1)}), bf16[4,2,65536]{2,1,0:T(2,128)(2,1)S(1)}, u32[]{:S(2)}, u32[]{:S(2)}) async-start(bf16[4,2,65536]{2,1,0:T(2,128)(2,1)} %reshape.81), calls=%async_computation.1 | async-start | bytes 2097152 | tf_op jit(solution)/shard_map/all_to_all | solution.py:79
  89.4 4.3 %collective-permute-start.2 = (f32[40,128]{1,0:T(8,128)S(1)}, f32[40,128]{1,0:T(8,128)S(1)}, u32[]{:S(2)}, u32[]{:S(2)}) collective-permute-start(f32[40,128]{1,0:T(8,128)S(1)} %get-tuple-element.8), channel_id=1, source_target_pairs={{1,0},{2,1},{3,2},{4,3},{5,4},{6,5},{7,6},{8,7},{9,8},{10,9},{11,1... | collective-permute-start | bytes 61448 | tf_op jit(solution)/shard_map/ppermute | solution.py:26
  91.3 6.0 %collective-permute-start.3 = (f32[40,128]{1,0:T(8,128)S(1)}, f32[40,128]{1,0:T(8,128)S(1)}, u32[]{:S(2)}, u32[]{:S(2)}) collective-permute-start(f32[40,128]{1,0:T(8,128)S(1)} %get-tuple-element.9), channel_id=1, source_target_pairs={{0,1},{1,2},{2,3},{3,4},{4,5},{5,6},{6,7},{7,8},{8,9},{9,10},{10,1... | collective-permute-start | bytes 61448 | tf_op jit(solution)/shard_map/ppermute | solution.py:26
where the time goes:
time: 117 us
  waiting for transfers between devices  63.9 us (55%)
  starting transfers between devices  17 us (15%)
  local copies, waits for them, and re-layouts  15.8 us (14%)
  matrix products  13.5 us (12%)
  other arithmetic  5.56 us (5%)
    all_to_all x1, waiting for transfers between devices, body(): lax.all_to_all(adjoint, 'harm', split_axis=1, concat_axis=0, tiled=True)  25.4 us
    ppermute x1, waiting for transfers between devices, with_halo(): after = lax.ppermute(initial, axis, down)  15.8 us
    all_to_all x1, waiting for transfers between devices, body(): lax.all_to_all(updated.reshape(harmonics, 1, node_count), 'harm', split_a...  14.8 us
    unnamed x22, local copies, waits for them, and re-layouts  8.93 us
    dot_general x1, matrix products, body(): jnp.einsum('kbsj,bsij->kbi', gathered, blocks, preferred_element_type=jnp...  6.17 us
    dot_general x1, matrix products, body(): radiative = jnp.dot(fourier.T, weighted, preferred_element_type=jnp.float32)  5.2 us
    all_to_all x1, starting transfers between devices, body(): lax.all_to_all(adjoint, 'harm', split_axis=1, concat_axis=0, tiled=True)  4.87 us
    ppermute x2, starting transfers between devices, passed_along(): lax.ppermute(value, axis, [(source, source + steps) for source in range(i...  4.33 us
  transfers between devices with their start and end apart: 6, of which 5 were waited for; matrix products, arithmetic and copies ran while one was open for 5% of the time, Pallas kernels for 0%

commit v1 on v0

--- a/solution.py
+++ b/solution.py
@@ -76,8 +76,16 @@
     ).reshape(harmonics, node_count)
     residual = source - (capacity[None, :] * rate_term + conduction + radiative)
     updated = (field.astype(jnp.float32) + inv_diag[None, :] * residual).astype(jnp.bfloat16)
-    returned = lax.all_to_all(
-        updated.reshape(harmonics, 1, node_count), "harm", split_axis=0, concat_axis=1, tiled=True
+    returned = jnp.concatenate(
+        lax.all_to_all(
+            jnp.stack(
+                jnp.split(updated.reshape(harmonics, 1, node_count), lax.axis_size("harm"), axis=0)
+            ),
+            "harm",
+            0,
+            0,
+        ),
+        axis=1,
     )
     weighted_terms = (updated.astype(jnp.float32) * heater_weight[None, :]).T
     window_zone = zone_of - (position - 1) * ZONE_DEV

time: 117 us -> 112 us (0.957)
  local copies, waits for them, and re-layouts: 15.8 us -> 12.4 us
  other arithmetic: 5.56 us -> 4.03 us
    unnamed x22 -> x19, local copies, waits for them, and re-layouts: 8.93 us -> 4.84 us
    reshape x1 -> x0, other arithmetic: 2.63 us -> none  [body(): updated.reshape(harmonics, 1, node_count)]
    another operation x0 -> x1, local copies, waits for them, and re-layouts: none -> 1.25 us  [body(): jnp.stack(jnp.split(updated.reshape(harmonics, 1, node_count), lax.axis_s...]
where the time goes in v1:
time: 112 us
  waiting for transfers between devices  63.9 us (57%)
  starting transfers between devices  17 us (15%)
  matrix products  13.5 us (12%)
  local copies, waits for them, and re-layouts  12.4 us (11%)
  other arithmetic  4.03 us (4%)
    all_to_all x1, waiting for transfers between devices, body(): lax.all_to_all(adjoint, 'harm', split_axis=1, concat_axis=0, tiled=True)  25.4 us
    ppermute x1, waiting for transfers between devices, with_halo(): after = lax.ppermute(initial, axis, down)  15.8 us
    all_to_all x1, waiting for transfers between devices, body(): lax.all_to_all(jnp.stack(jnp.split(updated.reshape(harmonics, 1, node_cou...  14.8 us
    dot_general x1, matrix products, body(): jnp.einsum('kbsj,bsij->kbi', gathered, blocks, preferred_element_type=jnp...  6.15 us
    dot_general x1, matrix products, body(): radiative = jnp.dot(fourier.T, weighted, preferred_element_type=jnp.float32)  5.21 us
    all_to_all x1, starting transfers between devices, body(): lax.all_to_all(adjoint, 'harm', split_axis=1, concat_axis=0, tiled=True)  4.87 us
    unnamed x19, local copies, waits for them, and re-layouts  4.84 us
    ppermute x2, starting transfers between devices, passed_along(): lax.ppermute(value, axis, [(source, source + steps) for source in range(i...  4.33 us
  transfers between devices with their start and end apart: 6, of which 5 were waited for; matrix products, arithmetic and copies ran while one was open for 5% of the time, Pallas kernels for 0%

profile of v1, /device:TPU:4, one launch (start us, length us, event | category | flops | bytes accessed | tf_op | source)
XLA Modules:
  0.0 111.7 jit_solution(12471242795779360121)
XLA Ops:
  0.6 0.0 copy-start.6
  0.6 2.8 %copy.26 = bf16[32,4,4096]{2,0,1:T(8,128)(2,1)} copy(bf16[32,4,4096]{2,1,0:T(4,128)(2,1)} %param.9) | data formatting | bytes 2097152 | tf_op args[0]
  3.4 4.9 %all-to-all-start = ((bf16[32,4,4096]{2,0,1:T(8,128)(2,1)}), bf16[32,4,4096]{2,0,1:T(8,128)(2,1)S(1)}, u32[]{:S(2)}, u32[]{:S(2)}) async-start(bf16[32,4,4096]{2,0,1:T(8,128)(2,1)} %copy.26), calls=%async_computation | async-start | bytes 2097152 | tf_op jit(solution)/shard_map/all_to_all | solution.py:58
  8.3 0.0 copy-done.6
  8.3 0.1 copy.31
  8.4 0.1 reshape.85
  8.5 0.1 copy.27
  8.6 25.4 %all-to-all-done = bf16[32,4,4096]{2,0,1:T(8,128)(2,1)S(1)} async-done(((bf16[32,4,4096]{2,0,1:T(8,128)(2,1)}), bf16[32,4,4096]{2,0,1:T(8,128)(2,1)S(1)}, u32[]{:S(2)}, u32[]{:S(2)}) %all-to-all-start) | async-done | bytes 1048608 | tf_op jit(solution)/shard_map/all_to_all | solution.py:58
  34.0 0.0 copy-start
  34.0 2.0 %collective-permute-start.1 = (bf16[128,4096]{1,0:T(8,128)(2,1)S(1)}, bf16[128,4096]{1,0:T(8,128)(2,1)S(1)}, u32[]{:S(2)}, u32[]{:S(2)}) collective-permute-start(bf16[128,4096]{1,0:T(8,128)(2,1)S(1)} %bitcast.44), channel_id=1, source_target_pairs={{1,0},{2,1},{3,2},{4,3},{5,4},{6,5},{7,6},{8,7},{9,8},{10,9},{11,1... | collective-permute-start | bytes 3145736 | tf_op jit(solution)/shard_map/ppermute | solution.py:18
  36.0 2.3 %collective-permute-start = (bf16[128,4096]{1,0:T(8,128)(2,1)S(1)}, bf16[128,4096]{1,0:T(8,128)(2,1)S(1)}, u32[]{:S(2)}, u32[]{:S(2)}) collective-permute-start(bf16[128,4096]{1,0:T(8,128)(2,1)S(1)} %bitcast.45), channel_id=1, source_target_pairs={{0,1},{1,2},{2,3},{3,4},{4,5},{5,6},{6,7},{7,8},{8,9},{9,10},{10,1... | collective-permute-start | bytes 3145736 | tf_op jit(solution)/shard_map/ppermute | solution.py:17
  38.3 0.3 bitcast_convert_fusion
  38.6 0.2 copy.37
  38.9 0.0 copy-done
  38.9 0.4 copy.29
  39.3 1.6 %slice_multiply_fusion.1 = (f32[63,4096]{1,0:T(8,128)}, f32[63,4096]{1,0:T(8,128)}) fusion(f32[128,4096]{1,0:T(8,128)S(1)} %bitcast_convert_fusion, f32[63]{0:T(128)S(1)} %get-tuple-element.18, f32[63]{0:T(128)S(1)} %get-tuple-element.19), kind=kLoop, calls=%fused_computation.24 | loop fusion | flops 516096 | bytes 4129272 | tf_op jit(solution)/shard_map/mul | solution.py:50
  40.9 15.8 %collective-permute-done.1 = bf16[128,4096]{1,0:T(8,128)(2,1)S(1)} collective-permute-done((bf16[128,4096]{1,0:T(8,128)(2,1)S(1)}, bf16[128,4096]{1,0:T(8,128)(2,1)S(1)}, u32[]{:S(2)}, u32[]{:S(2)}) %collective-permute-start.1) | collective-permute-done | bytes 1048608 | tf_op jit(solution)/shard_map/ppermute | solution.py:18
  56.7 0.3 copy_bitcast_fusion
  57.0 4.3 %collective-permute-done = bf16[128,4096]{1,0:T(8,128)(2,1)S(1)} collective-permute-done((bf16[128,4096]{1,0:T(8,128)(2,1)S(1)}, bf16[128,4096]{1,0:T(8,128)(2,1)S(1)}, u32[]{:S(2)}, u32[]{:S(2)}) %collective-permute-start) | collective-permute-done | bytes 1048608 | tf_op jit(solution)/shard_map/ppermute | solution.py:17
  61.4 0.3 copy_bitcast_fusion.1
  61.6 0.4 pad_maximum_fusion
  62.0 3.0 %gather_fusion = bf16[128,128,128]{2,1,0:T(8,128)(2,1)} fusion(bf16[128,96,128]{2,0,1:T(8,128)(2,1)S(1)} %pad_maximum_fusion, s32[1024]{0:T(1024)S(1)} %pad_clamp_fusion), kind=kCustom, calls=%fused_computation | custom fusion | bytes 8389120 | tf_op jit(solution)/shard_map/jit(_take)/gather | solution.py:73
  65.1 6.2 %fusion.5 = f32[32,128,128,1]{1,2,3,0:T(8,128)} fusion(bf16[32,4,128,128]{3,2,1,0:T(8,128)(2,1)} %param.14, bf16[32,4,128,128]{3,2,1,0:T(8,128)(2,1)} %bitcast.48, pred[32,4]{1,0:T(8,128)(4,1)S(1)} %copy.27), kind=kOutput, calls=%fused_computation.8 | convolution fusion | flops 538968064 | bytes 10485888 | tf_op jit(solution)/shard_map/kbsj,bsij->kbi/dot_general | solution.py:74
  71.2 0.0 copy-start.1
  71.2 0.0 copy-start.3
  71.2 0.0 copy-start.4
  71.2 2.0 %copy.32 = f32[128,4096]{1,0:T(8,128)S(1)} copy(f32[128,4096]{0,1:T(8,128)} %bitcast.51) | data formatting | bytes 4194304 | tf_op jit(solution)/shard_map/reshape | solution.py:76
  73.3 0.0 copy-done.1
  73.3 0.0 copy-done.3
  73.3 0.0 copy-done.4
  73.3 5.2 %fusion.4 = bf16[128,4096]{1,0:T(8,128)(2,1)} fusion(f32[128,4096]{1,0:T(8,128)} %param.10, f32[128,4096]{1,0:T(8,128)S(1)} %copy.32, f32[63,4096]{1,0:T(8,128)} %get-tuple-element.11, f32[1,4096]{1,0:T(1,128)S(1)} %broadcast_in_dim.41, f32[63,4096]{1,0:T(8,128)} %get-tuple-element.10, bf16[128,4096]{1,0:T(8,128)(2,1)S(1)} %bitcast.47, ...), kind=kOutput, calls=%fused_computation.7 | convolution fusion | flops 275939328 | bytes 9454720 | tf_op jit(solution)/shard_map/dot_general | solution.py:67
  78.5 1.3 %slice_bitcast_fusion.3 = (bf16[1,32,1,4096]{3,1,2,0:T(8,128)(2,1)S(1)}, bf16[1,32,1,4096]{3,1,2,0:T(8,128)(2,1)S(1)}, bf16[1,32,1,4096]{3,1,2,0:T(8,128)(2,1)S(1)}, bf16[1,32,1,4096]{3,1,2,0:T(8,128)(2,1)S(1)}) fusion(bf16[128,4096]{1,0:T(8,128)(2,1)} %fusion.4), kind=kLoop, calls=%fused_computation.31 | loop fusion | bytes 2097152 | tf_op jit(solution)/shard_map/stack | solution.py:81
  79.8 0.0 copy-start.5
  79.8 0.0 copy-start.2
  79.8 0.0 copy-start.7
  79.8 1.1 pad_maximum_fusion.1
  80.9 3.5 %all-to-all-start.1 = ((bf16[4,32,1,4096]{3,1,2,0:T(8,128)(2,1)}), bf16[4,32,1,4096]{3,1,2,0:T(8,128)(2,1)S(1)}, u32[]{:S(2)}, u32[]{:S(2)}) async-start(bf16[4,32,1,4096]{3,1,2,0:T(8,128)(2,1)} %pad_maximum_fusion.1), calls=%async_computation.1 | async-start | bytes 2097152 | tf_op jit(solution)/shard_map/all_to_all | solution.py:80
  84.4 0.0 copy-done.5
  84.5 0.0 copy-done.2
  84.5 0.0 copy-done.7
  84.5 2.1 %fusion.11 = f32[120,128]{1,0:T(8,128)S(1)} fusion(bf16[128,4096]{1,0:T(8,128)(2,1)S(1)} %copy-done.2, f32[4096]{0:T(1024)S(1)} %copy-done.7, s32[4096]{0:T(1024)S(1)} %broadcast_subtract_fusion), kind=kOutput, calls=%fused_computation.16 | convolution fusion | flops 757006336 | bytes 1142784 | tf_op jit(solution)/shard_map/nz,nk->zk/dot_general | solution.py:95
  86.6 1.9 %collective-permute-start.2 = (f32[40,128]{1,0:T(8,128)S(1)}, f32[40,128]{1,0:T(8,128)S(1)}, u32[]{:S(2)}, u32[]{:S(2)}) collective-permute-start(f32[40,128]{1,0:T(8,128)S(1)} %get-tuple-element.16), channel_id=1, source_target_pairs={{1,0},{2,1},{3,2},{4,3},{5,4},{6,5},{7,6},{8,7},{9,8},{10,9},{11,1... | collective-permute-start | bytes 61448 | tf_op jit(solution)/shard_map/ppermute | solution.py:26
  88.5 2.4 %collective-permute-start.3 = (f32[40,128]{1,0:T(8,128)S(1)}, f32[40,128]{1,0:T(8,128)S(1)}, u32[]{:S(2)}, u32[]{:S(2)}) collective-permute-start(f32[40,128]{1,0:T(8,128)S(1)} %get-tuple-element.17), channel_id=1, source_target_pairs={{0,1},{1,2},{2,3},{3,4},{4,5},{5,6},{6,7},{7,8},{8,9},{9,10},{10,1... | collective-permute-start | bytes 61448 | tf_op jit(solution)/shard_map/ppermute | solution.py:26
  90.9 0.0 collective-permute-done.2
  90.9 3.6 %collective-permute-done.3 = f32[40,128]{1,0:T(8,128)S(1)} collective-permute-done((f32[40,128]{1,0:T(8,128)S(1)}, f32[40,128]{1,0:T(8,128)S(1)}, u32[]{:S(2)}, u32[]{:S(2)}) %collective-permute-start.3) | collective-permute-done | bytes 20512 | tf_op jit(solution)/shard_map/ppermute | solution.py:26
  94.5 0.6 fusion.26
  95.1 14.8 %all-to-all-done.1 = bf16[4,32,1,4096]{3,1,2,0:T(8,128)(2,1)S(1)} async-done(((bf16[4,32,1,4096]{3,1,2,0:T(8,128)(2,1)}), bf16[4,32,1,4096]{3,1,2,0:T(8,128)(2,1)S(1)}, u32[]{:S(2)}, u32[]{:S(2)}) %all-to-all-start.1) | async-done | bytes 1048608 | tf_op jit(solution)/shard_map/all_to_all | solution.py:80
  109.9 1.8 %copy.33 = bf16[32,4,4096]{2,1,0:T(4,128)(2,1)} copy(bf16[32,4,4096]{2,0,1:T(8,128)(2,1)S(1)} %bitcast.49) | data formatting | bytes 2097152
  (8 shorter events, 0.1 us)
Async XLA Ops:
  0.6 7.7 %copy-start.6 = (s32[32,4]{0,1:T(4,128)S(1)}, s32[32,4]{0,1:T(4,128)}, u32[]{:S(2)}) copy-start(s32[32,4]{0,1:T(4,128)} %param.15) | copy-start | bytes 1540
  3.4 30.6 %all-to-all-start = ((bf16[32,4,4096]{2,0,1:T(8,128)(2,1)}), bf16[32,4,4096]{2,0,1:T(8,128)(2,1)S(1)}, u32[]{:S(2)}, u32[]{:S(2)}) async-start(bf16[32,4,4096]{2,0,1:T(8,128)(2,1)} %copy.26), calls=%async_computation | async-start | bytes 2097152 | tf_op jit(solution)/shard_map/all_to_all | solution.py:58
  34.0 4.9 %copy-start = (bf16[32,4,4096]{2,0,1:T(8,128)(2,1)}, bf16[32,4,4096]{2,0,1:T(8,128)(2,1)S(1)}, u32[]{:S(2)}) copy-start(bf16[32,4,4096]{2,0,1:T(8,128)(2,1)S(1)} %all-to-all-done) | copy-start | bytes 3145732
  34.0 22.7 %collective-permute-start.1 = (bf16[128,4096]{1,0:T(8,128)(2,1)S(1)}, bf16[128,4096]{1,0:T(8,128)(2,1)S(1)}, u32[]{:S(2)}, u32[]{:S(2)}) collective-permute-start(bf16[128,4096]{1,0:T(8,128)(2,1)S(1)} %bitcast.44), channel_id=1, source_target_pairs={{1,0},{2,1},{3,2},{4,3},{5,4},{6,5},{7,6},{8,7},{9,8},{10,9},{11,1... | collective-permute-start | bytes 3145736 | tf_op jit(solution)/shard_map/ppermute | solution.py:18
  36.0 25.3 %collective-permute-start = (bf16[128,4096]{1,0:T(8,128)(2,1)S(1)}, bf16[128,4096]{1,0:T(8,128)(2,1)S(1)}, u32[]{:S(2)}, u32[]{:S(2)}) collective-permute-start(bf16[128,4096]{1,0:T(8,128)(2,1)S(1)} %bitcast.45), channel_id=1, source_target_pairs={{0,1},{1,2},{2,3},{3,4},{4,5},{5,6},{6,7},{7,8},{8,9},{9,10},{10,1... | collective-permute-start | bytes 3145736 | tf_op jit(solution)/shard_map/ppermute | solution.py:17
  71.2 2.0 %copy-start.1 = (bf16[32,4,4096]{2,0,1:T(8,128)(2,1)S(1)}, bf16[32,4,4096]{2,0,1:T(8,128)(2,1)}, u32[]{:S(2)}) copy-start(bf16[32,4,4096]{2,0,1:T(8,128)(2,1)} %copy-done) | copy-start | bytes 3145732
  71.2 2.0 %copy-start.3 = (f32[4096]{0:T(1024)S(1)}, f32[4096]{0:T(1024)}, u32[]{:S(2)}) copy-start(f32[4096]{0:T(1024)} %param.12) | copy-start | bytes 49156
  71.2 2.1 %copy-start.4 = (f32[4096]{0:T(1024)S(1)}, f32[4096]{0:T(1024)}, u32[]{:S(2)}) copy-start(f32[4096]{0:T(1024)} %param.13) | copy-start | bytes 49156
  79.8 4.7 %copy-start.5 = (s32[4096]{0:T(1024)S(1)}, s32[4096]{0:T(1024)}, u32[]{:S(2)}) copy-start(s32[4096]{0:T(1024)} %param.16) | copy-start | bytes 49156
  79.8 4.7 %copy-start.2 = (bf16[128,4096]{1,0:T(8,128)(2,1)S(1)}, bf16[128,4096]{1,0:T(8,128)(2,1)}, u32[]{:S(2)}) copy-start(bf16[128,4096]{1,0:T(8,128)(2,1)} %fusion.4) | copy-start | bytes 3145732
  79.8 4.7 %copy-start.7 = (f32[4096]{0:T(1024)S(1)}, f32[4096]{0:T(1024)}, u32[]{:S(2)}) copy-start(f32[4096]{0:T(1024)} %param.17) | copy-start | bytes 49156
  80.9 29.0 %all-to-all-start.1 = ((bf16[4,32,1,4096]{3,1,2,0:T(8,128)(2,1)}), bf16[4,32,1,4096]{3,1,2,0:T(8,128)(2,1)S(1)}, u32[]{:S(2)}, u32[]{:S(2)}) async-start(bf16[4,32,1,4096]{3,1,2,0:T(8,128)(2,1)} %pad_maximum_fusion.1), calls=%async_computation.1 | async-start | bytes 2097152 | tf_op jit(solution)/shard_map/all_to_all | solution.py:80
  86.6 4.3 %collective-permute-start.2 = (f32[40,128]{1,0:T(8,128)S(1)}, f32[40,128]{1,0:T(8,128)S(1)}, u32[]{:S(2)}, u32[]{:S(2)}) collective-permute-start(f32[40,128]{1,0:T(8,128)S(1)} %get-tuple-element.16), channel_id=1, source_target_pairs={{1,0},{2,1},{3,2},{4,3},{5,4},{6,5},{7,6},{8,7},{9,8},{10,9},{11,1... | collective-permute-start | bytes 61448 | tf_op jit(solution)/shard_map/ppermute | solution.py:26
  88.5 6.0 %collective-permute-start.3 = (f32[40,128]{1,0:T(8,128)S(1)}, f32[40,128]{1,0:T(8,128)S(1)}, u32[]{:S(2)}, u32[]{:S(2)}) collective-permute-start(f32[40,128]{1,0:T(8,128)S(1)} %get-tuple-element.17), channel_id=1, source_target_pairs={{0,1},{1,2},{2,3},{3,4},{4,5},{5,6},{6,7},{7,8},{8,9},{9,10},{10,1... | collective-permute-start | bytes 61448 | tf_op jit(solution)/shard_map/ppermute | solution.py:26
